TPU v7x, 256 devices: a whole 4x4x8 slice. The times are simulated.
256 devices in a mesh: seq: 32 (over z, y_lo, core), mp: 8 (over x, y_hi).
Axes of the slice: x: 4, y: 4 (y_hi: 2, y_lo: 2; y = y_hi * 2 + y_lo), z: 8, core: 2. Of those that a mesh axis runs over, the one named last changes fastest.
Arguments:
- frames: bfloat16 [262144, 1024], P(('seq', 'mp')), may hold values from -6 to 6
- conv_kernel: float32 [31, 1024], replicated, may hold values from -1 to 1
- key_weight: bfloat16 [1024, 1024], P(None, 'mp'), may hold values from -0.1875 to 0.1875
- value_weight: bfloat16 [1024, 1024], P(None, 'mp'), may hold values from -0.1875 to 0.1875
- queries: bfloat16 [65536, 1024], P(('seq', 'mp')), may hold values from -512 to 512
- offsets: int32 [65536], P(('seq', 'mp')), may hold values from 0 to 261888, as said below
Outputs:
- context: bfloat16 [65536, 1024], P(('seq', 'mp'))
Inputs may be any that keep to these rules, and one draw needn't show every extreme that they name: offsets never fall; for the token at position t and i = t // 256, its band lies within frames i * 1024 - 512 to (i + 1) * 1024 + 511.
All inputs are finite; a program needn't handle non-finite values.
Results may differ from a plain program's by a relative error of at most 0.0075.
The roundings to bfloat16 on the way count: a program that leaves them out, or rounds other values in their place, can miss the bound.
Values may be sent and summed in bfloat16 or wider, within the bound.
A program may use at most 64 MiB of HBM per device.

v0:
```python
import jax
import jax.numpy as jnp
from jax import lax
from jax.sharding import PartitionSpec as P

HEAD_DIM = 64
BAND = 256


def shifted(value, axis, steps):
    count = lax.axis_size(axis)
    pairs = [(source, (source + steps) % count) for source in range(count)]
    return lax.ppermute(value, axis, pairs)


def extended(array, sides, width):
    for axis, dim in sides:
        devices, length = (lax.axis_size(axis), array.shape[dim])
        up = [(i, (i + 1) % devices) for i in range(devices - 1)]
        down = [(j, i) for i, j in up]
        last = lax.slice_in_dim(array, length - width, length, axis=dim)
        first = lax.slice_in_dim(array, 0, width, axis=dim)
        before = lax.ppermute(last, axis, up)
        after = lax.ppermute(first, axis, down)
        array = jnp.concatenate([before, array, after], axis=dim)
    return array


def place_panel(result, source, moving, anchor, panel_cols):
    product = jnp.einsum("rc,ncd->nrd", source, moving, preferred_element_type=jnp.float32).astype(
        jnp.bfloat16
    )
    return lax.dynamic_update_slice_in_dim(result, product, anchor * panel_cols, 2)


def project_rows(source, panels_pair):
    cycle_size = lax.axis_size("mp")
    own_index = lax.axis_index("mp")
    panel_cols = panels_pair.shape[2]
    result = jnp.zeros((2, source.shape[0], panel_cols * cycle_size), jnp.bfloat16)
    result = place_panel(result, source, panels_pair, own_index, panel_cols)
    moving = panels_pair
    for turn_index in range(1, cycle_size):
        moving = shifted(moving, "mp", 1)
        result = place_panel(
            result, source, moving, (own_index - turn_index) % cycle_size, panel_cols
        )
    return result


def band_context(queries, offsets, keys_values, first_frame):
    tok_rows = queries.shape[0]
    window = keys_values.shape[1]
    group_cols = 4 * HEAD_DIM
    group_count = queries.shape[1] // group_cols
    score_scale = HEAD_DIM ** (-0.5)
    band_start = offsets - first_frame
    frame_index = lax.broadcasted_iota(jnp.int32, (tok_rows, window), 1)
    inside = (frame_index >= band_start[:, None]) & (frame_index < band_start[:, None] + BAND)

    def attend_group(group_index):
        lower = group_index * group_cols
        query_part = lax.dynamic_slice_in_dim(queries, lower, group_cols, 1).reshape(
            tok_rows, 4, HEAD_DIM
        )
        key_part = lax.dynamic_slice_in_dim(keys_values[0], lower, group_cols, 1).reshape(
            window, 4, HEAD_DIM
        )
        value_part = lax.dynamic_slice_in_dim(keys_values[1], lower, group_cols, 1).reshape(
            window, 4, HEAD_DIM
        )
        scores = (
            jnp.einsum("thd,shd->hts", query_part, key_part, preferred_element_type=jnp.float32)
            * score_scale
        )
        scores = jnp.where(inside[None], scores, -jnp.inf)
        peak_score = jnp.max(scores, axis=2, keepdims=True)
        weights = jnp.exp(scores - peak_score)
        row_total = jnp.sum(weights, axis=2, keepdims=True)
        probability = (weights / row_total).astype(jnp.bfloat16)
        mixed_heads = jnp.einsum(
            "hts,shd->thd", probability, value_part, preferred_element_type=jnp.float32
        )
        return mixed_heads.reshape(tok_rows, group_cols)

    group_out = lax.map(attend_group, jnp.arange(group_count))
    return (
        jnp.transpose(group_out, (1, 0, 2))
        .reshape(tok_rows, group_count * group_cols)
        .astype(jnp.bfloat16)
    )


def shards(frames, conv_kernel, key_weight, value_weight, queries, offsets):
    local_rows = frames.shape[0]
    rim_width = (conv_kernel.shape[0] - 1) // 2
    reach_rows = local_rows // 2
    padded = extended(frames, ((("seq", "mp"), 0),), rim_width).astype(jnp.float32)
    mixed = jnp.zeros(frames.shape, jnp.float32)
    for offset_tap in range(conv_kernel.shape[0]):
        mixed = mixed + conv_kernel[offset_tap] * padded[offset_tap : offset_tap + local_rows]
    encoded = (frames.astype(jnp.float32) + jax.nn.silu(mixed)).astype(jnp.bfloat16)
    panels_pair = jnp.stack([key_weight, value_weight])
    own_keys = project_rows(encoded, panels_pair)
    keys_values = extended(own_keys, ((("seq", "mp"), 1),), reach_rows)
    first_frame = lax.axis_index(("seq", "mp")) * local_rows - reach_rows
    return band_context(queries, offsets, keys_values, first_frame)


def solution(mesh):
    return jax.shard_map(
        shards,
        mesh=mesh,
        in_specs=(
            P(("seq", "mp"), None),
            P(),
            P(None, "mp"),
            P(None, "mp"),
            P(("seq", "mp"), None),
            P(("seq", "mp")),
        ),
        out_specs=P(("seq", "mp"), None),
        check_vma=False,
    )
```

profile of v0, /device:TPU:65, one launch (start us, length us, event | category | flops | bytes accessed | tf_op | source)
XLA Modules:
  0.0 302.6 jit_solution(2885180084330778851)
XLA Ops:
  5.2 13.6 %collective-permute-done.2 = bf16[2,1024,128]{1,2,0:T(8,128)(2,1)S(1)} collective-permute-done((bf16[2,1024,128]{1,2,0:T(8,128)(2,1)S(1)}, bf16[2,1024,128]{1,2,0:T(8,128)(2,1)S(1)}, u32[]{:S(2)}, u32[]{:S(2)}) %collective-permute-start.2) | collective-permute-done | bytes 524320 | tf_op jit(solution)/shard_map/ppermute | solution.py:13
  19.5 14.9 %collective-permute-done.3 = bf16[2,1024,128]{1,2,0:T(8,128)(2,1)} collective-permute-done((bf16[2,1024,128]{1,2,0:T(8,128)(2,1)S(1)}, bf16[2,1024,128]{1,2,0:T(8,128)(2,1)}, u32[]{:S(2)}, u32[]{:S(2)}) %collective-permute-start.3) | collective-permute-done | bytes 524320 | tf_op jit(solution)/shard_map/ppermute | solution.py:13
  38.5 8.2 %collective-permute-start.1 = (bf16[15,1024]{1,0:T(8,128)(2,1)S(1)}, bf16[15,1024]{1,0:T(8,128)(2,1)S(1)}, u32[]{:S(2)}, u32[]{:S(2)}) collective-permute-start(bf16[15,1024]{1,0:T(8,128)(2,1)S(1)} %get-tuple-element.87), channel_id=1, source_target_pairs={{1,0},{2,1},{3,2},{4,3},{5,4},{6,5},{7,6},{8,7},{9,8},{10,9},{11,1... | collective-permute-start | bytes 92168 | tf_op jit(solution)/shard_map/ppermute | solution.py:24
  53.4 9.5 %concatenate.6 = bf16[1054,1024]{1,0:T(8,128)(2,1)S(1)} concatenate(bf16[15,1024]{1,0:T(8,128)(2,1)S(1)} %collective-permute-done, bf16[1024,1024]{1,0:T(8,128)(2,1)} %param.8, bf16[15,1024]{1,0:T(8,128)(2,1)S(1)} %collective-permute-done.1), dimensions={0} | concatenate | bytes 4317184 | tf_op jit(solution)/shard_map/concatenate | solution.py:25
  64.5 17.0 %add_convert_fusion = bf16[1024,1024]{1,0:T(8,128)(2,1)S(1)} fusion(bf16[1024,1024]{1,0:T(8,128)(2,1)S(1)} %copy-done.1, f32[1054,1024]{1,0:T(8,128)S(1)} %convert_element_type.70, f32[1024]{0:T(1024)S(1)} %bitcast.206, f32[1024]{0:T(1024)S(1)} %bitcast.207, f32[1024]{0:T(1024)S(1)} %bitcast.178, f32[1024]{0:T(1024)S(1)} %bitcast.179, ...), kind=kLoop, calls=%fused_computation.82 | loop fusion | flops 71303168 | bytes 134344704 | tf_op jit(solution)/shard_map/convert_element_type | solution.py:102
  85.5 13.9 %collective-permute-done.6 = bf16[2,1024,128]{1,2,0:T(8,128)(2,1)S(1)} collective-permute-done((bf16[2,1024,128]{1,2,0:T(8,128)(2,1)S(1)}, bf16[2,1024,128]{1,2,0:T(8,128)(2,1)S(1)}, u32[]{:S(2)}, u32[]{:S(2)}) %collective-permute-start.6) | collective-permute-done | bytes 524320 | tf_op jit(solution)/shard_map/ppermute | solution.py:13
  102.1 13.0 %collective-permute-done.7 = bf16[2,1024,128]{1,2,0:T(8,128)(2,1)S(1)} collective-permute-done((bf16[2,1024,128]{1,2,0:T(8,128)(2,1)S(1)}, bf16[2,1024,128]{1,2,0:T(8,128)(2,1)S(1)}, u32[]{:S(2)}, u32[]{:S(2)}) %collective-permute-start.7) | collective-permute-done | bytes 524320 | tf_op jit(solution)/shard_map/ppermute | solution.py:13
  116.6 13.2 %collective-permute-done.8 = bf16[2,1024,128]{1,2,0:T(8,128)(2,1)S(1)} collective-permute-done((bf16[2,1024,128]{1,2,0:T(8,128)(2,1)S(1)}, bf16[2,1024,128]{1,2,0:T(8,128)(2,1)S(1)}, u32[]{:S(2)}, u32[]{:S(2)}) %collective-permute-start.8) | collective-permute-done | bytes 524320 | tf_op jit(solution)/shard_map/ppermute | solution.py:13
  133.2 4.3 %collective-permute-start.10 = (bf16[2,512,1024]{1,2,0:T(8,128)(2,1)}, bf16[2,512,1024]{1,2,0:T(8,128)(2,1)}, u32[]{:S(2)}, u32[]{:S(2)}) collective-permute-start(bf16[2,512,1024]{1,2,0:T(8,128)(2,1)} %get-tuple-element.86), channel_id=1, source_target_pairs={{1,0},{2,1},{3,2},{4,3},{5,4},{6,5},{7,6},{8,7},{9,8},{10,9},{11,1... | collective-permute-start | bytes 6291464 | tf_op jit(solution)/shard_map/ppermute | solution.py:24
  140.1 85.6 %collective-permute-done.10 = bf16[2,512,1024]{1,2,0:T(8,128)(2,1)} collective-permute-done((bf16[2,512,1024]{1,2,0:T(8,128)(2,1)}, bf16[2,512,1024]{1,2,0:T(8,128)(2,1)}, u32[]{:S(2)}, u32[]{:S(2)}) %collective-permute-start.10) | collective-permute-done | bytes 2097184 | tf_op jit(solution)/shard_map/ppermute | solution.py:24
  225.7 7.2 %pad_maximum_fusion = bf16[2,2048,1024]{1,2,0:T(8,128)(2,1)} fusion(bf16[2,512,1024]{1,2,0:T(8,128)(2,1)} %collective-permute-done.10, bf16[2,1024,1024]{1,2,0:T(8,128)(2,1)} %copy-done, bf16[2,512,1024]{1,2,0:T(8,128)(2,1)} %collective-permute-done.9), kind=kLoop, calls=%fused_computation.20 | loop fusion | flops 25165824 | bytes 16777216 | tf_op jit(solution)/shard_map/concatenate | solution.py:25
  232.9 68.7 %while.11 = (s32[]{:T(128)}, bf16[4,256,256]{1,2,0:T(8,128)(2,1)S(1)}, bf16[2,2048,1024]{1,2,0:T(8,128)(2,1)}, s32[4]{0:T(128)S(1)}, bf16[256,1024]{1,0:T(8,128)...) while((s32[]{:T(128)}, ...), condition=%wide.region_3.4_spmd.clone, body=%wide.region_0.3_spmd.clone.sunk | while | flops 551028736 | bytes 41953456 | solution.py:86
  234.1 4.0 %fusion.159 = (bf16[1,2048,1024]{1,2,0:T(8,128)(2,1)S(1)}, bf16[1,2048,1024]{1,2,0:T(8,128)(2,1)S(1)}) fusion(bf16[2,2048,1024]{1,2,0:T(8,128)(2,1)} %get-tuple-element.199), kind=kLoop, calls=%fused_computation.126.clone.1 | loop fusion | bytes 16777216 | tf_op jit(solution)/shard_map/while/body/eval_jaxpr/slice | solution.py:66
  240.1 5.1 %fusion.161 = (f32[4,256]{1,0:T(4,128)S(1)}, f32[4,256,2048]{2,1,0:T(8,128)}) fusion(pred[256,2048]{1,0:T(8,128)(4,1)S(1)} %fusion.160, bf16[256,4,64]{0,2,1:T(8,128)(2,1)S(1)} %bitcast.170, bf16[2048,4,64]{0,2,1:T(8,128)(2,1)S(1)} %bitcast.169), kind=kOutput, calls=%fused_computation.127.clone.1 | convolution fusion | flops 276826112 | bytes 10096640 | tf_op jit(solution)/shard_map/while/body/eval_jaxpr/sub | solution.py:78
  245.2 4.8 %fusion.162 = bf16[4,64,256]{2,1,0:T(8,128)(2,1)S(1)} fusion(bf16[2048,4,64]{0,2,1:T(8,128)(2,1)S(1)} %bitcast.168, f32[4,256,2048]{2,1,0:T(8,128)} %get-tuple-element.173, f32[4,256]{1,0:T(4,128)S(1)} %get-tuple-element.174), kind=kOutput, calls=%fused_computation.9.clone.1 | convolution fusion | flops 272629760 | bytes 9572352 | tf_op jit(solution)/shard_map/while/body/eval_jaxpr/hts,shd->thd/dot_general | solution.py:81
  251.3 4.0 %fusion.159 = (bf16[1,2048,1024]{1,2,0:T(8,128)(2,1)S(1)}, bf16[1,2048,1024]{1,2,0:T(8,128)(2,1)S(1)}) fusion(bf16[2,2048,1024]{1,2,0:T(8,128)(2,1)} %get-tuple-element.199), kind=kLoop, calls=%fused_computation.126.clone.1 | loop fusion | bytes 16777216 | tf_op jit(solution)/shard_map/while/body/eval_jaxpr/slice | solution.py:66
  257.3 5.1 %fusion.161 = (f32[4,256]{1,0:T(4,128)S(1)}, f32[4,256,2048]{2,1,0:T(8,128)}) fusion(pred[256,2048]{1,0:T(8,128)(4,1)S(1)} %fusion.160, bf16[256,4,64]{0,2,1:T(8,128)(2,1)S(1)} %bitcast.170, bf16[2048,4,64]{0,2,1:T(8,128)(2,1)S(1)} %bitcast.169), kind=kOutput, calls=%fused_computation.127.clone.1 | convolution fusion | flops 276826112 | bytes 10096640 | tf_op jit(solution)/shard_map/while/body/eval_jaxpr/sub | solution.py:78
  262.4 4.8 %fusion.162 = bf16[4,64,256]{2,1,0:T(8,128)(2,1)S(1)} fusion(bf16[2048,4,64]{0,2,1:T(8,128)(2,1)S(1)} %bitcast.168, f32[4,256,2048]{2,1,0:T(8,128)} %get-tuple-element.173, f32[4,256]{1,0:T(4,128)S(1)} %get-tuple-element.174), kind=kOutput, calls=%fused_computation.9.clone.1 | convolution fusion | flops 272629760 | bytes 9572352 | tf_op jit(solution)/shard_map/while/body/eval_jaxpr/hts,shd->thd/dot_general | solution.py:81
  268.5 4.0 %fusion.159 = (bf16[1,2048,1024]{1,2,0:T(8,128)(2,1)S(1)}, bf16[1,2048,1024]{1,2,0:T(8,128)(2,1)S(1)}) fusion(bf16[2,2048,1024]{1,2,0:T(8,128)(2,1)} %get-tuple-element.199), kind=kLoop, calls=%fused_computation.126.clone.1 | loop fusion | bytes 16777216 | tf_op jit(solution)/shard_map/while/body/eval_jaxpr/slice | solution.py:66
  274.5 5.1 %fusion.161 = (f32[4,256]{1,0:T(4,128)S(1)}, f32[4,256,2048]{2,1,0:T(8,128)}) fusion(pred[256,2048]{1,0:T(8,128)(4,1)S(1)} %fusion.160, bf16[256,4,64]{0,2,1:T(8,128)(2,1)S(1)} %bitcast.170, bf16[2048,4,64]{0,2,1:T(8,128)(2,1)S(1)} %bitcast.169), kind=kOutput, calls=%fused_computation.127.clone.1 | convolution fusion | flops 276826112 | bytes 10096640 | tf_op jit(solution)/shard_map/while/body/eval_jaxpr/sub | solution.py:78
  279.5 4.8 %fusion.162 = bf16[4,64,256]{2,1,0:T(8,128)(2,1)S(1)} fusion(bf16[2048,4,64]{0,2,1:T(8,128)(2,1)S(1)} %bitcast.168, f32[4,256,2048]{2,1,0:T(8,128)} %get-tuple-element.173, f32[4,256]{1,0:T(4,128)S(1)} %get-tuple-element.174), kind=kOutput, calls=%fused_computation.9.clone.1 | convolution fusion | flops 272629760 | bytes 9572352 | tf_op jit(solution)/shard_map/while/body/eval_jaxpr/hts,shd->thd/dot_general | solution.py:81
  285.6 4.0 %fusion.159 = (bf16[1,2048,1024]{1,2,0:T(8,128)(2,1)S(1)}, bf16[1,2048,1024]{1,2,0:T(8,128)(2,1)S(1)}) fusion(bf16[2,2048,1024]{1,2,0:T(8,128)(2,1)} %get-tuple-element.199), kind=kLoop, calls=%fused_computation.126.clone.1 | loop fusion | bytes 16777216 | tf_op jit(solution)/shard_map/while/body/eval_jaxpr/slice | solution.py:66
  291.6 5.1 %fusion.161 = (f32[4,256]{1,0:T(4,128)S(1)}, f32[4,256,2048]{2,1,0:T(8,128)}) fusion(pred[256,2048]{1,0:T(8,128)(4,1)S(1)} %fusion.160, bf16[256,4,64]{0,2,1:T(8,128)(2,1)S(1)} %bitcast.170, bf16[2048,4,64]{0,2,1:T(8,128)(2,1)S(1)} %bitcast.169), kind=kOutput, calls=%fused_computation.127.clone.1 | convolution fusion | flops 276826112 | bytes 10096640 | tf_op jit(solution)/shard_map/while/body/eval_jaxpr/sub | solution.py:78
  296.7 4.8 %fusion.162 = bf16[4,64,256]{2,1,0:T(8,128)(2,1)S(1)} fusion(bf16[2048,4,64]{0,2,1:T(8,128)(2,1)S(1)} %bitcast.168, f32[4,256,2048]{2,1,0:T(8,128)} %get-tuple-element.173, f32[4,256]{1,0:T(4,128)S(1)} %get-tuple-element.174), kind=kOutput, calls=%fused_computation.9.clone.1 | convolution fusion | flops 272629760 | bytes 9572352 | tf_op jit(solution)/shard_map/while/body/eval_jaxpr/hts,shd->thd/dot_general | solution.py:81
  (65 shorter events, 43.3 us)
Async XLA Ops:
  2.2 16.6 %collective-permute-start.2 = (bf16[2,1024,128]{1,2,0:T(8,128)(2,1)S(1)}, bf16[2,1024,128]{1,2,0:T(8,128)(2,1)S(1)}, u32[]{:S(2)}, u32[]{:S(2)}) collective-permute-start(bf16[2,1024,128]{1,2,0:T(8,128)(2,1)S(1)} %pad_maximum_fusion.1), channel_id=1, source_target_pairs={{0,1},{1,2},{2,3},{3,4},{4,5},{5,6},{6,7},{7,0},{8,9},{9,10},{10,1... | collective-permute-start | bytes 1572872 | tf_op jit(solution)/shard_map/ppermute | solution.py:13
  18.8 15.6 %collective-permute-start.3 = (bf16[2,1024,128]{1,2,0:T(8,128)(2,1)S(1)}, bf16[2,1024,128]{1,2,0:T(8,128)(2,1)}, u32[]{:S(2)}, u32[]{:S(2)}) collective-permute-start(bf16[2,1024,128]{1,2,0:T(8,128)(2,1)S(1)} %collective-permute-done.2), channel_id=1, source_target_pairs={{0,1},{1,2},{2,3},{3,4},{4,5},{5,6},{6,7},{7,0},{8,9},{9,10},{10,1... | collective-permute-start | bytes 1572872 | tf_op jit(solution)/shard_map/ppermute | solution.py:13
  34.4 29.0 %collective-permute-start.4 = (bf16[2,1024,128]{1,2,0:T(8,128)(2,1)}, bf16[2,1024,128]{1,2,0:T(8,128)(2,1)}, u32[]{:S(2)}, u32[]{:S(2)}) collective-permute-start(bf16[2,1024,128]{1,2,0:T(8,128)(2,1)} %collective-permute-done.3), channel_id=1, source_target_pairs={{0,1},{1,2},{2,3},{3,4},{4,5},{5,6},{6,7},{7,0},{8,9},{9,10},{10,1... | collective-permute-start | bytes 1572872 | tf_op jit(solution)/shard_map/ppermute | solution.py:13
  35.2 17.5 %collective-permute-start = (bf16[15,1024]{1,0:T(8,128)(2,1)S(1)}, bf16[15,1024]{1,0:T(8,128)(2,1)S(1)}, u32[]{:S(2)}, u32[]{:S(2)}) collective-permute-start(bf16[15,1024]{1,0:T(8,128)(2,1)S(1)} %get-tuple-element.88), channel_id=1, source_target_pairs={{0,1},{1,2},{2,3},{3,4},{4,5},{5,6},{6,7},{7,8},{8,9},{9,10},{10,1... | collective-permute-start | bytes 92168 | tf_op jit(solution)/shard_map/ppermute | solution.py:23
  38.5 14.9 %collective-permute-start.1 = (bf16[15,1024]{1,0:T(8,128)(2,1)S(1)}, bf16[15,1024]{1,0:T(8,128)(2,1)S(1)}, u32[]{:S(2)}, u32[]{:S(2)}) collective-permute-start(bf16[15,1024]{1,0:T(8,128)(2,1)S(1)} %get-tuple-element.87), channel_id=1, source_target_pairs={{1,0},{2,1},{3,2},{4,3},{5,4},{6,5},{7,6},{8,7},{9,8},{10,9},{11,1... | collective-permute-start | bytes 92168 | tf_op jit(solution)/shard_map/ppermute | solution.py:24
  62.9 1.6 copy-start.1
  63.4 19.4 %collective-permute-start.5 = (bf16[2,1024,128]{1,2,0:T(8,128)(2,1)}, bf16[2,1024,128]{1,2,0:T(8,128)(2,1)S(1)}, u32[]{:S(2)}, u32[]{:S(2)}) collective-permute-start(bf16[2,1024,128]{1,2,0:T(8,128)(2,1)} %collective-permute-done.4), channel_id=1, source_target_pairs={{0,1},{1,2},{2,3},{3,4},{4,5},{5,6},{6,7},{7,0},{8,9},{9,10},{10,1... | collective-permute-start | bytes 1572872 | tf_op jit(solution)/shard_map/ppermute | solution.py:13
  82.9 16.6 %collective-permute-start.6 = (bf16[2,1024,128]{1,2,0:T(8,128)(2,1)S(1)}, bf16[2,1024,128]{1,2,0:T(8,128)(2,1)S(1)}, u32[]{:S(2)}, u32[]{:S(2)}) collective-permute-start(bf16[2,1024,128]{1,2,0:T(8,128)(2,1)S(1)} %collective-permute-done.5), channel_id=1, source_target_pairs={{0,1},{1,2},{2,3},{3,4},{4,5},{5,6},{6,7},{7,0},{8,9},{9,10},{10,1... | collective-permute-start | bytes 1572872 | tf_op jit(solution)/shard_map/ppermute | solution.py:13
  99.5 15.6 %collective-permute-start.7 = (bf16[2,1024,128]{1,2,0:T(8,128)(2,1)S(1)}, bf16[2,1024,128]{1,2,0:T(8,128)(2,1)S(1)}, u32[]{:S(2)}, u32[]{:S(2)}) collective-permute-start(bf16[2,1024,128]{1,2,0:T(8,128)(2,1)S(1)} %collective-permute-done.6), channel_id=1, source_target_pairs={{0,1},{1,2},{2,3},{3,4},{4,5},{5,6},{6,7},{7,0},{8,9},{9,10},{10,1... | collective-permute-start | bytes 1572872 | tf_op jit(solution)/shard_map/ppermute | solution.py:13
  115.1 14.7 %collective-permute-start.8 = (bf16[2,1024,128]{1,2,0:T(8,128)(2,1)S(1)}, bf16[2,1024,128]{1,2,0:T(8,128)(2,1)S(1)}, u32[]{:S(2)}, u32[]{:S(2)}) collective-permute-start(bf16[2,1024,128]{1,2,0:T(8,128)(2,1)S(1)} %collective-permute-done.7), channel_id=1, source_target_pairs={{0,1},{1,2},{2,3},{3,4},{4,5},{5,6},{6,7},{7,0},{8,9},{9,10},{10,1... | collective-permute-start | bytes 1572872 | tf_op jit(solution)/shard_map/ppermute | solution.py:13
  130.6 2.7 copy-start
  130.6 9.5 %copy-start.2 = (s32[256]{0:T(256)S(1)}, s32[256]{0:T(256)}, u32[]{:S(2)}) copy-start(s32[256]{0:T(256)} %param.13) | copy-start | bytes 3076
  133.2 92.5 %collective-permute-start.10 = (bf16[2,512,1024]{1,2,0:T(8,128)(2,1)}, bf16[2,512,1024]{1,2,0:T(8,128)(2,1)}, u32[]{:S(2)}, u32[]{:S(2)}) collective-permute-start(bf16[2,512,1024]{1,2,0:T(8,128)(2,1)} %get-tuple-element.86), channel_id=1, source_target_pairs={{1,0},{2,1},{3,2},{4,3},{5,4},{6,5},{7,6},{8,7},{9,8},{10,9},{11,1... | collective-permute-start | bytes 6291464 | tf_op jit(solution)/shard_map/ppermute | solution.py:24
  137.5 88.2 %collective-permute-start.9 = (bf16[2,512,1024]{1,2,0:T(8,128)(2,1)S(1)}, bf16[2,512,1024]{1,2,0:T(8,128)(2,1)}, u32[]{:S(2)}, u32[]{:S(2)}) collective-permute-start(bf16[2,512,1024]{1,2,0:T(8,128)(2,1)S(1)} %get-tuple-element.85), channel_id=1, source_target_pairs={{0,1},{1,2},{2,3},{3,4},{4,5},{5,6},{6,7},{7,8},{8,9},{9,10},{10,1... | collective-permute-start | bytes 6291464 | tf_op jit(solution)/shard_map/ppermute | solution.py:23
where the time goes:
time: 307 us; the launch traced here: 303 us
  waiting for transfers between devices  158 us (51%)
  matrix products  47.8 us (16%)
  local copies, waits for them, and re-layouts  43.2 us (14%)
  other arithmetic  27.8 us (9%)
  starting transfers between devices  22.2 us (7%)
    ppermute x2, waiting for transfers between devices, extended(): after = lax.ppermute(first, axis, down)  86.4 us
    ppermute x7, waiting for transfers between devices, shifted(): return lax.ppermute(value, axis, pairs)  68.6 us
    sub x4, matrix products, attend_group(): weights = jnp.exp(scores - peak_score)  20.3 us
    dot_general x4, matrix products, attend_group(): jnp.einsum('hts,shd->thd', probability, value_part, preferred_element_typ...  19.3 us
    convert_element_type x1, other arithmetic, shards(): (frames.astype(jnp.float32) + jax.nn.silu(mixed)).astype(jnp.bfloat16)  17 us
    slice x4, local copies, waits for them, and re-layouts, attend_group(): keys_values[0]  16 us
    ppermute x2, starting transfers between devices, extended(): after = lax.ppermute(first, axis, down)  12.5 us
    concatenate x1, local copies, waits for them, and re-layouts, extended(): array = jnp.concatenate([before, array, after], axis=dim)  9.49 us
  transfers between devices with their start and end apart: 11, of which 8 were waited for; matrix products, arithmetic and copies ran while one was open for 13% of the time, Pallas kernels for 0%

commit v1 on v0

v1 whole, which is shorter than its diff:
```python
import jax
import jax.numpy as jnp
from jax import lax
from jax.experimental import pallas as pl
from jax.experimental.pallas import tpu as pltpu
from jax.sharding import PartitionSpec as P

BF = jnp.bfloat16
F32 = jnp.float32
MESH = pl.DeviceIdType.MESH

HEAD_DIM = 64
BAND = 256
ROWS = 1024
TOKS = 256
WIDTH = 1024
LANES = 128
BLOCKS = WIDTH // LANES
TAPS = 31
HALF = ROWS // 2
HALO = 16
TILE = 128
PACK = LANES + 16
CHUNKS = 4
CCOLS = WIDTH // CHUNKS
NEG = -1e30
SCALE2 = HEAD_DIM ** -0.5 * 1.4426950408889634
MERGE_LAG = 2


def kernel(
    frames, taps, key_panel, value_panel, queries, offs,
    out,
    xpad, enc, wbuf, kbuf, vbuf, hbuf, offown, offn, qn, bias, biasn,
    part, oret, osend, pret, msend, ctx, stat,
    halo_s, halo_r, off_s, off_r, q_s, q_r, f_s, f_r,
    w_s, w_r, b_s, b_r, o_s, o_r, p_s, p_r,
):
    seq, mp = lax.axis_index("seq"), lax.axis_index("mp")
    me = seq * 8 + mp
    x, hi = mp // 2, mp % 2
    core, lo = seq % 2, (seq // 2) % 2
    sign = 1 - 2 * hi

    def at(index):
        wrapped = lax.rem(index + 256, 256)
        return {"seq": wrapped // 8, "mp": lax.rem(wrapped, 8)}

    up, down = at(me + 1), at(me - 1)
    partner = {"seq": seq, "mp": mp + sign}
    other = at(me - sign)
    onward = at(me + 2 * sign)
    source = at(me - 2 * sign)
    sibling = {"seq": seq + 1 - 2 * core, "mp": mp}
    across = {"seq": seq + 2 - 4 * lo, "mp": mp + sign}
    xplus = {"seq": seq, "mp": lax.rem(mp + 2, 8)}
    xminus = {"seq": seq, "mp": lax.rem(mp + 6, 8)}
    relay = {"seq": seq, "mp": lax.rem(mp + 6 + 4 * hi, 8)}

    def copy(src, dst, send, recv, device):
        return pltpu.make_async_remote_copy(
            src_ref=src, dst_ref=dst, send_sem=send, recv_sem=recv, device_id=device, device_id_type=MESH
        )

    def panel_of(r):
        g = r // 2
        step = g + (g // 2) * (5 - 2 * g)
        flip = lax.rem(r + hi, 2)
        return lax.rem(x + step, 4) * 2 + flip

    slot_p, slot_o = 1 - hi, hi

    halo_up = copy(frames.at[pl.ds(ROWS - HALO, HALO)], hbuf.at[0], halo_s.at[0], halo_r.at[0], up)
    halo_down = copy(frames.at[pl.ds(0, HALO)], hbuf.at[1], halo_s.at[1], halo_r.at[1], down)
    off_p = copy(offown, offn.at[hi], off_s.at[0], off_r.at[hi], partner)
    off_o = copy(offown, offn.at[1 - hi], off_s.at[1], off_r.at[1 - hi], other)

    def q_copy(c):
        cols = pl.ds(c * CCOLS, CCOLS)
        return copy(queries.at[:, cols], qn.at[hi, :, cols], q_s.at[c], q_r.at[c], partner)

    def q_arrival(c):
        cols = pl.ds(c * CCOLS, CCOLS)
        dst = qn.at[slot_p, :, cols]
        return copy(dst, dst, q_s.at[c], q_r.at[c], partner)

    def f_copy(c):
        cols = pl.ds(c * CCOLS, CCOLS)
        return copy(qn.at[slot_p, :, cols], qn.at[hi, :, cols], f_s.at[c], f_r.at[c], onward)

    def f_arrival(c):
        cols = pl.ds(c * CCOLS, CCOLS)
        dst = qn.at[slot_o, :, cols]
        return copy(dst, dst, f_s.at[c], f_r.at[c], source)

    def w_copy(n, src, dst, device):
        return copy(wbuf.at[src, core], wbuf.at[dst, core], w_s.at[n], w_r.at[dst], device)

    own_across = w_copy(0, 0, 1, across)
    own_xplus = w_copy(1, 0, 4, xplus)
    own_xminus = w_copy(2, 0, 2, xminus)
    next_xplus = w_copy(3, 1, 5, xplus)
    next_xminus = w_copy(4, 1, 3, xminus)
    relay_own = w_copy(5, 2 + 2 * hi, 6, relay)
    relay_next = w_copy(6, 3 + 2 * hi, 7, relay)

    def w_arrival(r):
        dst = wbuf.at[r, core]
        return copy(dst, dst, w_s.at[0], w_r.at[r], across)

    def b_copy(r):
        return copy(wbuf.at[r, core], wbuf.at[r, core], b_s.at[r], b_r.at[r], sibling)

    def b_arrival(r):
        dst = wbuf.at[r, 1 - core]
        return copy(dst, dst, b_s.at[r], b_r.at[r], sibling)

    def o_copy(a):
        return copy(osend.at[a], oret.at[a], o_s.at[a], o_r.at[a], source)

    def p_copy(a):
        return copy(msend.at[a], pret.at[a], p_s.at[a], p_r.at[a], partner)

    barrier = pltpu.get_barrier_semaphore()
    greeted = (up, down, onward, source, sibling, across, xplus, xminus)
    for device in greeted:
        pl.semaphore_signal(barrier, inc=1, device_id=device, device_id_type=MESH)
    offown[...] = jnp.broadcast_to(offs[...], (8, TOKS))
    wbuf[0, 0] = key_panel[...]
    wbuf[0, 1] = value_panel[...]
    pl.semaphore_wait(barrier, len(greeted))

    halo_up.start()
    halo_down.start()
    own_across.start()
    off_p.start()
    off_o.start()
    own_xplus.start()
    own_xminus.start()
    for c in range(CHUNKS):
        q_copy(c).start()

    def band_bias(ref, first, row):
        count = ref.shape[0]

        def fill(n, _):
            rows = pl.ds(pl.multiple_of(n * 128, 128), 128)
            frame = first + n * 128 + lax.broadcasted_iota(jnp.int32, (128, TOKS), 0)
            gap = frame - row
            ref[rows, :] = jnp.where((gap & -BAND) == 0, 0.0, NEG)
            return 0

        lax.fori_loop(0, count // 128, fill, 0)

    band_bias(bias, me * ROWS, offown[0:1, :])

    halo_up.wait_recv()
    halo_down.wait_recv()

    def after_block(b):
        @pl.when(b == 1)
        def _():
            q_arrival(0).wait_recv()
            f_copy(0).start()

        @pl.when(b == 3)
        def _():
            w_arrival(1).wait_recv()
            next_xplus.start()
            next_xminus.start()
            b_copy(1).start()
            q_arrival(1).wait_recv()
            f_copy(1).start()

        @pl.when(b == 4)
        def _():
            w_arrival(2).wait_recv()
            b_copy(2).start()
            w_arrival(4).wait_recv()
            b_copy(4).start()
            relay_own.start()

        @pl.when(b == 5)
        def _():
            q_arrival(2).wait_recv()
            f_copy(2).start()

        @pl.when(b == 7)
        def _():
            q_arrival(3).wait_recv()
            f_copy(3).start()
            w_arrival(3).wait_recv()
            b_copy(3).start()
            w_arrival(5).wait_recv()
            b_copy(5).start()
            relay_next.start()

    def conv_block(b, _):
        cols = pl.ds(pl.multiple_of(b * LANES, LANES), LANES)
        xpad[pl.ds(0, HALO), :] = jnp.where(me > 0, hbuf[0, :, cols].astype(F32), 0.0)
        xpad[pl.ds(HALO, ROWS), :] = frames[:, cols].astype(F32)
        xpad[pl.ds(HALO + ROWS, HALO), :] = jnp.where(me < 255, hbuf[1, :, cols].astype(F32), 0.0)

        def tile(t, _):
            top = pl.multiple_of(t * TILE, TILE)
            acc = jnp.zeros((TILE, LANES), F32)
            for phase in range(8):
                window = xpad[pl.ds(top + phase + 1, TILE + 24), :]
                for k in range(phase, TAPS, 8):
                    acc = acc + taps[pl.ds(k, 1), cols] * window[k - phase : k - phase + TILE]
            here = xpad[pl.ds(top + HALO, TILE), :]
            half = 0.5 * acc
            enc[pl.ds(top, TILE), cols] = (here + (half + half * jnp.tanh(half))).astype(BF)
            return 0

        lax.fori_loop(0, ROWS // TILE, tile, 0)
        after_block(b)
        return 0

    lax.fori_loop(0, BLOCKS, conv_block, 0)

    def project(r, _):
        @pl.when(r == 2)
        def _():
            w_arrival(6).wait_recv()
            b_copy(6).start()

        @pl.when(r == 4)
        def _():
            w_arrival(7).wait_recv()
            b_copy(7).start()

        @pl.when(r > 0)
        def _():
            b_arrival(r).wait_recv()

        a = panel_of(r)

        def rows_part(n, _):
            rows = pl.ds(pl.multiple_of(n * HALF, HALF), HALF)
            weight = jnp.concatenate([wbuf[r, 0], wbuf[r, 1]], axis=1)
            both = jnp.dot(enc[rows, :], weight, preferred_element_type=F32)
            kbuf[a, rows, :] = both[:, :LANES].astype(BF)
            vbuf[a, :, rows] = both[:, LANES:].T.astype(BF)
            return 0

        lax.fori_loop(0, 2, rows_part, 0)
        return 0

    lax.fori_loop(0, BLOCKS, project, 0)

    lane = lax.broadcasted_iota(jnp.int32, (TOKS, LANES), 1)

    def attend(q, keys, values_t, mask):
        result = []
        for h in range(2):
            inside = (lane >= h * HEAD_DIM) & (lane < (h + 1) * HEAD_DIM)
            masked_q = jnp.where(inside, q.astype(F32), 0.0).astype(BF)
            scores = lax.dot_general(
                keys, masked_q, (((1,), (1,)), ((), ())), preferred_element_type=F32
            ) + mask
            peak = jnp.max(scores, axis=0, keepdims=True)
            weights = jnp.exp2((scores - peak) * SCALE2)
            total = jnp.sum(weights, axis=0, keepdims=True)
            mixed = jnp.dot(
                values_t[h * HEAD_DIM : (h + 1) * HEAD_DIM], weights.astype(BF), preferred_element_type=F32
            )
            result.append((mixed, peak, total))
        return result

    def three(v):
        first = v.astype(BF).astype(F32)
        second = (v - first).astype(BF).astype(F32)
        return [first, second, (v - first) - second]

    def attend_remote(a, slot, target):
        cols = pl.ds(pl.multiple_of(a * LANES, LANES), LANES)
        part_rows = pl.ds(pl.multiple_of(slot * HALF, HALF), HALF)
        heads = attend(qn[slot, :, cols], kbuf[a, part_rows, :], vbuf[a, :, part_rows], biasn[slot])
        rows = []
        for h, (mixed, peak, total) in enumerate(heads):
            target[a, h * HEAD_DIM : (h + 1) * HEAD_DIM, :] = (mixed / total).astype(BF)
            rows += three(peak) + three(total)
        rows.append(jnp.zeros((4, TOKS), F32))
        target[a, LANES:, :] = jnp.concatenate(rows, axis=0).astype(BF)

    def merge(a):
        o_copy(a).wait_recv()
        theirs = oret[a].astype(F32)
        mine = part[a].astype(F32)
        msend[a] = jnp.where(theirs[LANES : LANES + 1] > 0.1 * NEG, theirs, mine).astype(BF)
        p_copy(a).start()

    for slot in range(2):
        copy(offn.at[slot], offn.at[slot], off_s.at[slot], off_r.at[slot], partner).wait_recv()
        band_bias(biasn.at[slot], me * ROWS + slot * HALF, offn[slot, 0:1, :])

    def remote_step(a, _):
        @pl.when(a % 2 == 0)
        def _():
            f_arrival(a // 2).wait_recv()

        attend_remote(a, slot_o, osend)
        o_copy(a).start()
        attend_remote(a, slot_p, part)

        @pl.when(a >= MERGE_LAG)
        def _():
            merge(a - MERGE_LAG)

        return 0

    lax.fori_loop(0, BLOCKS, remote_step, 0)

    def own_step(a, _):
        cols = pl.ds(pl.multiple_of(a * LANES, LANES), LANES)
        heads = attend(queries[:, cols], kbuf[a], vbuf[a], bias[...])
        rows = []
        for h, (mixed, peak, total) in enumerate(heads):
            ctx[a, h * HEAD_DIM : (h + 1) * HEAD_DIM, :] = mixed
            rows += [peak, total]
        rows.append(jnp.zeros((4, TOKS), F32))
        stat[a] = jnp.concatenate(rows, axis=0)

        @pl.when(a < MERGE_LAG)
        def _():
            merge(a + BLOCKS - MERGE_LAG)

        return 0

    lax.fori_loop(0, BLOCKS, own_step, 0)

    def final_step(a, _):
        cols = pl.ds(pl.multiple_of(a * LANES, LANES), LANES)
        p_copy(a).wait_recv()
        far_rows = pret[a, LANES:, :].astype(F32)
        parts = []
        for h in range(2):
            far_peak = far_rows[6 * h : 6 * h + 1] + far_rows[6 * h + 1 : 6 * h + 2] + far_rows[6 * h + 2 : 6 * h + 3]
            far_total = far_rows[6 * h + 3 : 6 * h + 4] + far_rows[6 * h + 4 : 6 * h + 5] + far_rows[6 * h + 5 : 6 * h + 6]
            peak, total = stat[a, 2 * h : 2 * h + 1, :], stat[a, 2 * h + 1 : 2 * h + 2, :]
            top = jnp.maximum(peak, far_peak)
            near_weight = jnp.exp2((peak - top) * SCALE2)
            far_weight = jnp.exp2((far_peak - top) * SCALE2) * far_total
            scale = 1.0 / (near_weight * total + far_weight)
            head_rows = slice(h * HEAD_DIM, (h + 1) * HEAD_DIM)
            parts.append(
                ctx[a, head_rows, :] * (near_weight * scale) + pret[a, head_rows, :].astype(F32) * (far_weight * scale)
            )
        out[:, cols] = jnp.concatenate(parts, axis=0).T.astype(BF)
        return 0

    lax.fori_loop(0, BLOCKS, final_step, 0)

    for sent in (
        halo_up, halo_down, off_p, off_o, own_across, own_xplus, own_xminus,
        next_xplus, next_xminus, relay_own, relay_next,
    ):
        sent.wait_send()
    for c in range(CHUNKS):
        q_copy(c).wait_send()
        f_copy(c).wait_send()

    def drain(a, _):
        o_copy(a).wait_send()
        p_copy(a).wait_send()

        @pl.when(a > 0)
        def _():
            b_copy(a).wait_send()

        return 0

    lax.fori_loop(0, BLOCKS, drain, 0)


def shards(frames, conv_kernel, key_weight, value_weight, queries, offsets):
    dma = pltpu.SemaphoreType.DMA
    whole = pl.BlockSpec(memory_space=pltpu.VMEM)
    return pl.pallas_call(
        kernel,
        out_shape=jax.ShapeDtypeStruct((TOKS, WIDTH), BF),
        in_specs=[whole] * 6,
        out_specs=whole,
        scratch_shapes=[
            pltpu.VMEM((ROWS + 2 * HALO + 8, LANES), F32),
            pltpu.VMEM((ROWS, WIDTH), BF),
            pltpu.VMEM((BLOCKS, 2, WIDTH, LANES), BF),
            pltpu.VMEM((BLOCKS, ROWS, LANES), BF),
            pltpu.VMEM((BLOCKS, LANES, ROWS), BF),
            pltpu.VMEM((2, HALO, WIDTH), BF),
            pltpu.VMEM((8, TOKS), jnp.int32),
            pltpu.VMEM((2, 8, TOKS), jnp.int32),
            pltpu.VMEM((2, TOKS, WIDTH), BF),
            pltpu.VMEM((ROWS, TOKS), F32),
            pltpu.VMEM((2, HALF, TOKS), F32),
            pltpu.VMEM((BLOCKS, PACK, TOKS), BF),
            pltpu.VMEM((BLOCKS, PACK, TOKS), BF),
            pltpu.VMEM((BLOCKS, PACK, TOKS), BF),
            pltpu.VMEM((BLOCKS, PACK, TOKS), BF),
            pltpu.VMEM((BLOCKS, PACK, TOKS), BF),
            pltpu.VMEM((BLOCKS, LANES, TOKS), F32),
            pltpu.VMEM((BLOCKS, 8, TOKS), F32),
            dma((2,)), dma((2,)), dma((2,)), dma((2,)),
            dma((CHUNKS,)), dma((CHUNKS,)), dma((CHUNKS,)), dma((CHUNKS,)),
            dma((7,)), dma((8,)), dma((8,)), dma((8,)),
            dma((BLOCKS,)), dma((BLOCKS,)), dma((BLOCKS,)), dma((BLOCKS,)),
        ],
        compiler_params=pltpu.CompilerParams(
            collective_id=0, has_side_effects=True, vmem_limit_bytes=48 * 1024 * 1024
        ),
        cost_estimate=pl.CostEstimate(
            flops=9_000_000_000, bytes_accessed=4_500_000, transcendentals=10_000_000
        ),
        name="speech_window",
    )(frames, conv_kernel, key_weight, value_weight, queries, offsets.reshape(1, TOKS))


def solution(mesh):
    return jax.shard_map(
        shards,
        mesh=mesh,
        in_specs=(
            P(("seq", "mp"), None),
            P(),
            P(None, "mp"),
            P(None, "mp"),
            P(("seq", "mp"), None),
            P(("seq", "mp")),
        ),
        out_specs=P(("seq", "mp"), None),
        check_vma=False,
    )
```

time: 307 us -> 88.2 us (0.29)
  the two profiles are of different devices: /device:TPU:65 before, /device:TPU:16 now
where the time goes in v1:
time: 88.2 us; the launch traced here: 88 us
  Pallas kernels  81 us (92%)
  local copies, waits for them, and re-layouts  6.91 us (8%)
    pallas_call x1, Pallas kernels, shards(): pl.pallas_call(kernel, out_shape=jax.ShapeDtypeStruct((TOKS, WIDTH), BF),...  81 us
    unnamed x13, local copies, waits for them, and re-layouts  6.91 us

profile of v1, /device:TPU:16, one launch (start us, length us, event | category | flops | bytes accessed | tf_op | source)
XLA Modules:
  0.0 88.0 jit_solution(10733365964734792576)
XLA Ops:
  0.0 0.0 copy-start
  0.0 1.6 %copy-done = bf16[1024,1024]{1,0:T(8,128)(2,1)S(1)} copy-done((bf16[1024,1024]{1,0:T(8,128)(2,1)S(1)}, bf16[1024,1024]{1,0:T(8,128)(2,1)}, u32[]{:S(2)}) %copy-start) | copy-done | bytes 2097176
  1.6 0.0 copy-start.1
  1.6 1.0 %copy-done.1 = bf16[256,1024]{1,0:T(8,128)(2,1)S(1)} copy-done((bf16[256,1024]{1,0:T(8,128)(2,1)S(1)}, bf16[256,1024]{1,0:T(8,128)(2,1)}, u32[]{:S(2)}) %copy-start.1) | copy-done | bytes 524312
  2.6 0.0 copy-start.2
  2.6 0.9 %copy-done.2 = bf16[1024,128]{1,0:T(8,128)(2,1)S(1)} copy-done((bf16[1024,128]{1,0:T(8,128)(2,1)S(1)}, bf16[1024,128]{1,0:T(8,128)(2,1)}, u32[]{:S(2)}) %copy-start.2) | copy-done | bytes 262168
  3.6 0.0 copy-start.3
  3.6 0.9 %copy-done.3 = bf16[1024,128]{1,0:T(8,128)(2,1)S(1)} copy-done((bf16[1024,128]{1,0:T(8,128)(2,1)S(1)}, bf16[1024,128]{1,0:T(8,128)(2,1)}, u32[]{:S(2)}) %copy-start.3) | copy-done | bytes 262168
  4.5 0.0 copy-start.4
  4.5 0.9 %copy-done.4 = f32[31,1024]{1,0:T(8,128)S(1)} copy-done((f32[31,1024]{1,0:T(8,128)S(1)}, f32[31,1024]{1,0:T(8,128)}, u32[]{:S(2)}) %copy-start.4) | copy-done | bytes 127000
  5.4 0.0 copy-start.5
  5.4 0.7 copy-done.5
  6.1 81.0 %speech_window.1 = bf16[256,1024]{1,0:T(8,128)(2,1)S(1)} custom-call(bf16[1024,1024]{1,0:T(8,128)(2,1)S(1)} %copy-done, f32[31,1024]{1,0:T(8,128)S(1)} %copy-done.4, bf16[1024,128]{1,0:T(8,128)(2,1)S(1)} %copy-done.2, bf16[1024,128]{1,0:T(8,128)(2,1)S(1)} %copy-done.3, bf16[256,1024]{1,0:T(8,128)(2,1)S(1)} %copy-done.1, s32[1,256]{1,0:T(1,128)S(1)} %bitcast.1), custom_call_target="tpu_custom_call" | custom-call | flops 8999999488 | bytes 4500000 | tf_op jit(solution)/shard_map/speech_window/pallas_call | solution.py:380
  87.2 0.8 copy.8
Async XLA Ops:
  0.0 1.6 %copy-start = (bf16[1024,1024]{1,0:T(8,128)(2,1)S(1)}, bf16[1024,1024]{1,0:T(8,128)(2,1)}, u32[]{:S(2)}) copy-start(bf16[1024,1024]{1,0:T(8,128)(2,1)} %frames.1) | copy-start | bytes 6291460
  1.6 1.0 %copy-start.1 = (bf16[256,1024]{1,0:T(8,128)(2,1)S(1)}, bf16[256,1024]{1,0:T(8,128)(2,1)}, u32[]{:S(2)}) copy-start(bf16[256,1024]{1,0:T(8,128)(2,1)} %queries.1) | copy-start | bytes 1572868
  2.6 0.9 %copy-start.2 = (bf16[1024,128]{1,0:T(8,128)(2,1)S(1)}, bf16[1024,128]{1,0:T(8,128)(2,1)}, u32[]{:S(2)}) copy-start(bf16[1024,128]{1,0:T(8,128)(2,1)} %key_panel.1) | copy-start | bytes 786436
  3.6 0.9 %copy-start.3 = (bf16[1024,128]{1,0:T(8,128)(2,1)S(1)}, bf16[1024,128]{1,0:T(8,128)(2,1)}, u32[]{:S(2)}) copy-start(bf16[1024,128]{1,0:T(8,128)(2,1)} %value_panel.1) | copy-start | bytes 786436
  4.5 0.9 %copy-start.4 = (f32[31,1024]{1,0:T(8,128)S(1)}, f32[31,1024]{1,0:T(8,128)}, u32[]{:S(2)}) copy-start(f32[31,1024]{1,0:T(8,128)} %taps.1) | copy-start | bytes 380932
  5.4 0.7 copy-start.5

commit v2 on v1

v2 whole, which is shorter than its diff:
```python
import jax
import jax.numpy as jnp
from jax import lax
from jax.experimental import pallas as pl
from jax.experimental.pallas import tpu as pltpu
from jax.sharding import PartitionSpec as P

BF = jnp.bfloat16
F32 = jnp.float32
MESH = pl.DeviceIdType.MESH

HEAD_DIM = 64
BAND = 256
ROWS = 1024
TOKS = 256
WIDTH = 1024
LANES = 128
BLOCKS = WIDTH // LANES
TAPS = 31
HALF = ROWS // 2
HALO = 16
TILE = 256
VROWS = HEAD_DIM + 16
PACK = LANES + 16
CHUNKS = 4
CCOLS = WIDTH // CHUNKS
NEG = -1e30
SCALE2 = HEAD_DIM ** -0.5 * 1.4426950408889634
FETCH_AT = 4
OPEN_AT = 0


def kernel(
    frames_in, taps_in, key_panel, value_panel, queries_in, offs_in,
    out,
    frames, taps, queries, offs, edge, xpad, wtap, score0, score1, prob0, prob1, enc, wbuf, kbuf, vbuf, hbuf, offown, offn, qn, bias, biasn,
    part, oret, pret, msend, ctx, stat, near,
    in_s, halo_s, halo_r, off_s, off_r, q_s, q_r, f_s, f_r,
    w_s, w_r, z_s, z_r, b_s, b_r, c_s, c_r, o_s, o_r, p_s, p_r,
):
    seq, mp = lax.axis_index("seq"), lax.axis_index("mp")
    me = seq * 8 + mp
    x, hi = mp // 2, mp % 2
    core, lo, kind = seq % 2, (seq // 2) % 2, (seq // 4) % 2
    sign = 1 - 2 * hi

    def at(index):
        wrapped = lax.rem(index + 256, 256)
        return {"seq": wrapped // 8, "mp": lax.rem(wrapped, 8)}

    up, down = at(me + 1), at(me - 1)
    partner = {"seq": seq, "mp": mp + sign}
    other = at(me - sign)
    onward = at(me + 2 * sign)
    source = at(me - 2 * sign)
    sibling = {"seq": seq + 1 - 2 * core, "mp": mp}
    across = {"seq": seq + 2 - 4 * lo, "mp": mp + sign}
    xplus = {"seq": seq, "mp": lax.rem(mp + 2, 8)}
    xminus = {"seq": seq, "mp": lax.rem(mp + 6, 8)}
    zplus = {"seq": lax.rem(seq + 4, 32), "mp": mp}
    zminus = {"seq": lax.rem(seq + 28, 32), "mp": mp}
    relay = {"seq": seq, "mp": lax.rem(mp + 6 + 4 * hi, 8)}

    def copy(src, dst, send, recv, device):
        return pltpu.make_async_remote_copy(
            src_ref=src, dst_ref=dst, send_sem=send, recv_sem=recv, device_id=device, device_id_type=MESH
        )

    def turn(step):
        return lax.rem(x + sign * step + 16, CHUNKS)

    def chunk_of(g):
        return turn(g + (g // 2) * (5 - 2 * g))

    def piece_of(g):
        return 2 * g + 2 * hi * ((g % 2) * (1 - g // 2) - (g // 2) * (1 - g % 2))

    slot_p, slot_o = 1 - hi, hi

    halo_up = copy(frames_in.at[pl.ds(ROWS - HALO, HALO)], hbuf.at[0], halo_s.at[0], halo_r.at[0], up)
    halo_down = copy(frames_in.at[pl.ds(0, HALO)], hbuf.at[1], halo_s.at[1], halo_r.at[1], down)
    off_p = copy(offown, offn.at[hi], off_s.at[0], off_r.at[hi], partner)
    off_o = copy(offown, offn.at[1 - hi], off_s.at[1], off_r.at[1 - hi], other)

    def q_copy(c):
        cols = pl.ds(c * CCOLS, CCOLS)
        return copy(queries_in.at[:, cols], qn.at[hi, :, cols], q_s.at[c], q_r.at[c], partner)

    def q_arrival(c):
        cols = pl.ds(c * CCOLS, CCOLS)
        dst = qn.at[slot_p, :, cols]
        return copy(dst, dst, q_s.at[c], q_r.at[c], partner)

    def f_copy(c):
        cols = pl.ds(c * CCOLS, CCOLS)
        return copy(qn.at[slot_p, :, cols], qn.at[hi, :, cols], f_s.at[c], f_r.at[c], onward)

    def f_arrival(c):
        cols = pl.ds(c * CCOLS, CCOLS)
        dst = qn.at[slot_o, :, cols]
        return copy(dst, dst, f_s.at[c], f_r.at[c], source)

    def piece(r, kv, half):
        return wbuf.at[r, kv, pl.ds(pl.multiple_of(half * HALF, HALF), HALF)]

    def w_copy(n, src, dst, device):
        return copy(piece(src, kind, core), piece(dst, kind, core), w_s.at[n], w_r.at[dst], device)

    own_across = w_copy(0, 0, 1, across)
    own_xplus = w_copy(1, 0, 4, xplus)
    own_xminus = w_copy(2, 0, 2, xminus)
    next_xplus = w_copy(3, 1, 5, xplus)
    next_xminus = w_copy(4, 1, 3, xminus)
    relay_own = w_copy(5, 2 + 2 * hi, 6, relay)
    relay_next = w_copy(6, 3 + 2 * hi, 7, relay)

    def w_arrival(r):
        dst = piece(r, kind, core)
        return copy(dst, dst, w_s.at[0], w_r.at[r], across)

    def z_copy(r, odd):
        src = piece(r, kind, core)
        return copy(src, src, z_s.at[r], z_r.at[r], zminus if odd else zplus)

    def z_arrival(r):
        dst = piece(r, 1 - kind, core)
        return copy(dst, dst, z_s.at[r], z_r.at[r], zplus)

    def b_copy(r):
        src = piece(r, kind, core)
        return copy(src, src, b_s.at[r], b_r.at[r], sibling)

    def b_arrival(r):
        dst = piece(r, kind, 1 - core)
        return copy(dst, dst, b_s.at[r], b_r.at[r], sibling)

    def c_copy(r):
        src = piece(r, 1 - kind, core)
        return copy(src, src, c_s.at[r], c_r.at[r], sibling)

    def c_arrival(r):
        dst = piece(r, 1 - kind, 1 - core)
        return copy(dst, dst, c_s.at[r], c_r.at[r], sibling)

    def fetched(r, odd):
        w_arrival(r).wait_recv()
        z_copy(r, odd).start()
        b_copy(r).start()

    def passed(r):
        z_arrival(r).wait_recv()
        c_copy(r).start()

    def onward_queries(c):
        q_arrival(c).wait_recv()
        f_copy(c).start()

    def o_copy(a):
        return copy(part.at[slot_o, a], oret.at[a], o_s.at[a], o_r.at[a], source)

    def p_copy(a):
        return copy(msend.at[a], pret.at[a], p_s.at[a], p_r.at[a], partner)

    barrier = pltpu.get_barrier_semaphore()
    greeted = (up, down, onward, source, sibling, across, xplus, xminus, zplus, zminus)
    for device in greeted:
        pl.semaphore_signal(barrier, inc=1, device_id=device, device_id_type=MESH)
    inputs = [
        pltpu.make_async_copy(src, dst, in_s.at[n])
        for n, (src, dst) in enumerate((
            (frames_in, frames), (taps_in, taps), (offs_in, offs),
            (key_panel, wbuf.at[0, 0]), (value_panel, wbuf.at[0, 1]), (queries_in, queries),
        ))
    ]
    for load in inputs:
        load.start()
    xpad[pl.ds(0, HALO), :] = jnp.zeros((HALO, LANES), F32)
    xpad[pl.ds(HALO + ROWS, HALO), :] = jnp.zeros((HALO, LANES), F32)
    for h in range(2):
        vbuf[:, h, HEAD_DIM:, :] = jnp.ones((BLOCKS, VROWS - HEAD_DIM, ROWS), BF)
    for load in inputs:
        load.wait()
    offown[...] = jnp.broadcast_to(offs[...], (8, TOKS))

    def open_up():
        pl.semaphore_wait(barrier, len(greeted))
        own_across.start()
        own_xplus.start()
        own_xminus.start()
        halo_up.start()
        halo_down.start()
        off_p.start()
        off_o.start()

    def band_bias(ref, first, row):
        count = ref.shape[0]

        def fill(n, _):
            rows = pl.ds(pl.multiple_of(n * 128, 128), 128)
            frame = first + n * 128 + lax.broadcasted_iota(jnp.int32, (128, TOKS), 0)
            gap = frame - row
            ref[rows, :] = jnp.where((gap & -BAND) == 0, 0.0, NEG)
            return 0

        lax.fori_loop(0, count // 128, fill, 0)

    band_bias(bias, me * ROWS, offown[0:1, :])

    def after_block(b):
        @pl.when(b == OPEN_AT)
        def _():
            open_up()

        @pl.when(b == FETCH_AT)
        def _():
            fetched(1, True)
            next_xplus.start()
            next_xminus.start()
            fetched(2 + 2 * hi, False)
            relay_own.start()
            fetched(4 - 2 * hi, False)
            for step in (0, -1, -2, -3):
                q_copy(turn(step)).start()

        @pl.when(b == 6)
        def _():
            passed(1)

        @pl.when(b == 7)
        def _():
            fetched(3 + 2 * hi, True)
            relay_next.start()
            fetched(5 - 2 * hi, True)
            onward_queries(turn(0))

    def convolve(source_ref, top, count, b):
        acc = jnp.zeros((count // 8, 8, LANES), F32)
        for phase in range(8):
            window = source_ref[pl.ds(top + phase + 1, count + 24), :].reshape(count // 8 + 3, 8, LANES)
            for k in range(phase, TAPS, 8):
                acc = acc + wtap[b, k] * window[k // 8 : k // 8 + count // 8]
        half = 0.5 * acc.reshape(count, LANES)
        here = source_ref[pl.ds(top + HALO, count), :]
        return (here + (half + half * jnp.tanh(half))).astype(BF)

    def conv_block(b, _):
        cols = pl.ds(pl.multiple_of(b * LANES, LANES), LANES)
        xpad[pl.ds(HALO, ROWS), :] = frames[:, cols].astype(F32)
        for k in range(TAPS):
            wtap[b, k] = jnp.broadcast_to(taps[pl.ds(k, 1), cols], (8, LANES))

        def tile(t, _):
            top = pl.multiple_of(t * TILE, TILE)
            enc[pl.ds(top, TILE), cols] = convolve(xpad, top, TILE, b)
            return 0

        lax.fori_loop(0, ROWS // TILE, tile, 0)
        after_block(b)
        return 0

    lax.fori_loop(0, BLOCKS, conv_block, 0)

    halo_up.wait_recv()
    halo_down.wait_recv()

    def edge_block(b, _):
        cols = pl.ds(pl.multiple_of(b * LANES, LANES), LANES)
        edge[0, :HALO, :] = jnp.where(me > 0, hbuf[0, :, cols].astype(F32), 0.0)
        edge[0, HALO:, :] = frames[: 2 * HALO, cols].astype(F32)
        edge[1, : 2 * HALO, :] = frames[ROWS - 2 * HALO :, cols].astype(F32)
        edge[1, 2 * HALO :, :] = jnp.where(me < 255, hbuf[1, :, cols].astype(F32), 0.0)
        enc[:HALO, cols] = convolve(edge.at[0], 0, HALO, b)
        enc[ROWS - HALO :, cols] = convolve(edge.at[1], 0, HALO, b)
        return 0

    lax.fori_loop(0, BLOCKS, edge_block, 0)

    for slot in range(2):
        copy(offn.at[slot], offn.at[slot], off_s.at[slot], off_r.at[slot], partner).wait_recv()
        band_bias(biasn.at[slot], me * ROWS + slot * HALF, offn[slot, 0:1, :])

    def project(r, a):
        weight = jnp.concatenate([wbuf[r, 0], wbuf[r, 1]], axis=1)
        both = jnp.dot(enc[...], weight, preferred_element_type=F32)
        kbuf[a] = both[:, :LANES].astype(BF)
        turned = both[:, LANES:].T.astype(BF)
        for h in range(2):
            vbuf[a, h, :HEAD_DIM, :] = turned[h * HEAD_DIM : (h + 1) * HEAD_DIM]

    def project_chunk(g):
        def one(k, _):
            r = piece_of(g) + k

            @pl.when(r > 0)
            def _():
                b_arrival(r).wait_recv()
                c_arrival(r).wait_recv()

            project(r, chunk_of(g) * 2 + lax.rem(hi + k, 2))
            return 0

        lax.fori_loop(0, 2, one, 0)

    lane = lax.broadcasted_iota(jnp.int32, (TOKS, LANES), 1)
    halves = (pl.ds(0, HALF), pl.ds(HALF, HALF))

    def head_queries(q, h):
        inside = (lane >= h * HEAD_DIM) & (lane < (h + 1) * HEAD_DIM)
        return jnp.where(inside, q.astype(F32), 0.0).astype(BF)

    def score(keys, q, h, mask, target):
        scores = lax.dot_general(
            keys, head_queries(q, h), (((1,), (1,)), ((), ())), preferred_element_type=F32
        ) + mask
        target[...] = scores
        return jnp.max(scores, axis=0, keepdims=True)

    def weigh(scores, peak, target):
        target[...] = jnp.exp2((scores[...] - peak) * SCALE2).astype(BF)

    def mix(values, weights):
        mixed = jnp.dot(values, weights, preferred_element_type=F32)
        return mixed[:HEAD_DIM], mixed[HEAD_DIM : HEAD_DIM + 1]

    score_refs, prob_refs = (score0, score1), (prob0, prob1)

    def three(v):
        first = v.astype(BF).astype(F32)
        second = (v - first).astype(BF).astype(F32)
        return [first, second, (v - first) - second]

    def panel_cols(a):
        return pl.ds(pl.multiple_of(a * LANES, LANES), LANES)

    def remote_score(a, h):
        return tuple(
            score(kbuf[a, halves[n], :], qn[n, :, panel_cols(a)], h, biasn[n], score_refs[h].at[halves[n]])
            for n in range(2)
        )

    def remote_weigh(h, peaks):
        for n in range(2):
            weigh(score_refs[h].at[halves[n]], peaks[n], prob_refs[h].at[halves[n]])

    def remote_mix(a, h, peaks):
        for n in range(2):
            mixed, total = mix(vbuf[a, h, :, halves[n]], prob_refs[h][halves[n], :])
            part[n, a, h * HEAD_DIM : (h + 1) * HEAD_DIM, :] = (mixed / total).astype(BF)
            rows = three(peaks[n]) + three(total) + [jnp.zeros((2, TOKS), F32)]
            stat[n, a, 8 * h : 8 * h + 8, :] = jnp.concatenate(rows, axis=0)

    def remote_pack(a):
        for n in range(2):
            part[n, a, LANES:, :] = stat[n, a].astype(BF)

    def merge(a):
        o_copy(a).wait_recv()
        theirs = oret[a].astype(F32)
        mine = part[slot_p, a].astype(F32)
        msend[a] = jnp.where(theirs[LANES : LANES + 1] > 0.1 * NEG, theirs, mine).astype(BF)
        p_copy(a).start()

    def merge_chunk(c):
        def one(k, _):
            merge(2 * c + k)
            return 0

        lax.fori_loop(0, 2, one, 0)

    def remote_chunk(c):
        peaks = remote_score(2 * c, 0)
        for k in range(2):
            a = 2 * c + k
            peaks1 = remote_score(a, 1)
            remote_weigh(0, peaks)
            remote_mix(a, 0, peaks)
            if k == 0:
                later = remote_score(a + 1, 0)
            remote_weigh(1, peaks1)
            remote_mix(a, 1, peaks1)
            remote_pack(a)
            o_copy(a).start()
            peaks = later

    def chunk_step(g, _):
        @pl.when(g == 0)
        def _():
            passed(2 + 2 * hi)
            passed(3 + 2 * hi)

        @pl.when(g == 1)
        def _():
            onward_queries(turn(-1))
            passed(4 - 2 * hi)
            passed(5 - 2 * hi)
            fetched(6, False)
            fetched(7, True)

        @pl.when(g == 2)
        def _():
            passed(6)
            passed(7)

        @pl.when(g < CHUNKS - 1)
        def _():
            project_chunk(g + 1)

        @pl.when(g == 0)
        def _():
            onward_queries(turn(2))

        f_arrival(chunk_of(g)).wait_recv()
        remote_chunk(chunk_of(g))

        @pl.when(g == 1)
        def _():
            merge_chunk(turn(1))

        @pl.when(g == 3)
        def _():
            merge_chunk(turn(0))
            merge_chunk(turn(2))

        return 0

    project_chunk(0)
    onward_queries(turn(1))
    lax.fori_loop(0, CHUNKS, chunk_step, 0)

    def own_score(a, h):
        return score(kbuf[a], queries[:, panel_cols(a)], h, bias[...], score_refs[h])

    def own_mix(a, h, peak):
        mixed, total = mix(vbuf[a, h], prob_refs[h][...])
        ctx[a, h * HEAD_DIM : (h + 1) * HEAD_DIM, :] = mixed
        near[a, 8 * h : 8 * h + 8, :] = jnp.concatenate([peak, total, jnp.zeros((6, TOKS), F32)], axis=0)

    def own_step(a, peak0):
        peak1 = own_score(a, 1)
        weigh(score0, peak0, prob0)
        own_mix(a, 0, peak0)
        peak_next = own_score(jnp.minimum(a + 1, BLOCKS - 1), 0)
        weigh(score1, peak1, prob1)
        own_mix(a, 1, peak1)

        @pl.when(a == 1)
        def _():
            merge_chunk(turn(-1))

        return peak_next

    lax.fori_loop(0, BLOCKS, own_step, own_score(0, 0))

    def final_step(a, _):
        cols = pl.ds(pl.multiple_of(a * LANES, LANES), LANES)
        p_copy(a).wait_recv()
        far_rows = pret[a, LANES:, :].astype(F32)
        parts = []
        for h in range(2):
            far_peak = sum(far_rows[8 * h + n : 8 * h + n + 1] for n in range(3))
            far_total = sum(far_rows[8 * h + n : 8 * h + n + 1] for n in range(3, 6))
            peak, total = near[a, 8 * h : 8 * h + 1, :], near[a, 8 * h + 1 : 8 * h + 2, :]
            top = jnp.maximum(peak, far_peak)
            near_weight = jnp.exp2((peak - top) * SCALE2)
            far_weight = jnp.exp2((far_peak - top) * SCALE2) * far_total
            scale = 1.0 / (near_weight * total + far_weight)
            head_rows = slice(h * HEAD_DIM, (h + 1) * HEAD_DIM)
            parts.append(
                ctx[a, head_rows, :] * (near_weight * scale) + pret[a, head_rows, :].astype(F32) * (far_weight * scale)
            )
        out[:, cols] = jnp.concatenate(parts, axis=0).T.astype(BF)
        return 0

    for step in (-1, 0, 2, 1):
        first = 2 * turn(step)
        lax.fori_loop(first, first + 2, final_step, 0)

    for sent in (
        halo_up, halo_down, off_p, off_o, own_across, own_xplus, own_xminus,
        next_xplus, next_xminus, relay_own, relay_next,
    ):
        sent.wait_send()
    for c in range(CHUNKS):
        q_copy(c).wait_send()
        f_copy(c).wait_send()

    for r in range(1, BLOCKS):
        z_copy(r, r % 2).wait_send()
        b_copy(r).wait_send()
        c_copy(r).wait_send()

    def drain(a, _):
        o_copy(a).wait_send()
        p_copy(a).wait_send()

        return 0

    lax.fori_loop(0, BLOCKS, drain, 0)


def shards(frames, conv_kernel, key_weight, value_weight, queries, offsets):
    dma = pltpu.SemaphoreType.DMA
    whole = pl.BlockSpec(memory_space=pltpu.VMEM)
    far = pl.BlockSpec(memory_space=pltpu.HBM)
    return pl.pallas_call(
        kernel,
        out_shape=jax.ShapeDtypeStruct((TOKS, WIDTH), BF),
        in_specs=[far] * 6,
        out_specs=whole,
        scratch_shapes=[
            pltpu.VMEM((ROWS, WIDTH), BF),
            pltpu.VMEM((TAPS, WIDTH), F32),
            pltpu.VMEM((TOKS, WIDTH), BF),
            pltpu.VMEM((1, TOKS), jnp.int32),
            pltpu.VMEM((2, 3 * HALO, LANES), F32),
            pltpu.VMEM((ROWS + 2 * HALO, LANES), F32),
            pltpu.VMEM((BLOCKS, TAPS, 8, LANES), F32),
            pltpu.VMEM((ROWS, TOKS), F32),
            pltpu.VMEM((ROWS, TOKS), F32),
            pltpu.VMEM((ROWS, TOKS), BF),
            pltpu.VMEM((ROWS, TOKS), BF),
            pltpu.VMEM((ROWS, WIDTH), BF),
            pltpu.VMEM((BLOCKS, 2, WIDTH, LANES), BF),
            pltpu.VMEM((BLOCKS, ROWS, LANES), BF),
            pltpu.VMEM((BLOCKS, 2, VROWS, ROWS), BF),
            pltpu.VMEM((2, HALO, WIDTH), BF),
            pltpu.VMEM((8, TOKS), jnp.int32),
            pltpu.VMEM((2, 8, TOKS), jnp.int32),
            pltpu.VMEM((2, TOKS, WIDTH), BF),
            pltpu.VMEM((ROWS, TOKS), F32),
            pltpu.VMEM((2, HALF, TOKS), F32),
            pltpu.VMEM((2, BLOCKS, PACK, TOKS), BF),
            pltpu.VMEM((BLOCKS, PACK, TOKS), BF),
            pltpu.VMEM((BLOCKS, PACK, TOKS), BF),
            pltpu.VMEM((BLOCKS, PACK, TOKS), BF),
            pltpu.VMEM((BLOCKS, LANES, TOKS), F32),
            pltpu.VMEM((2, BLOCKS, 16, TOKS), F32),
            pltpu.VMEM((BLOCKS, 16, TOKS), F32),
            dma((6,)), dma((2,)), dma((2,)), dma((2,)), dma((2,)),
            dma((CHUNKS,)), dma((CHUNKS,)), dma((CHUNKS,)), dma((CHUNKS,)),
            dma((7,)), dma((8,)), dma((8,)), dma((8,)), dma((8,)), dma((8,)), dma((8,)), dma((8,)),
            dma((BLOCKS,)), dma((BLOCKS,)), dma((BLOCKS,)), dma((BLOCKS,)),
        ],
        compiler_params=pltpu.CompilerParams(
            collective_id=0, has_side_effects=True, vmem_limit_bytes=63 * 1024 * 1024
        ),
        cost_estimate=pl.CostEstimate(
            flops=9_000_000_000, bytes_accessed=4_500_000, transcendentals=10_000_000
        ),
        name="speech_window",
    )(frames, conv_kernel, key_weight, value_weight, queries, offsets.reshape(1, TOKS))


def solution(mesh):
    return jax.shard_map(
        shards,
        mesh=mesh,
        in_specs=(
            P(("seq", "mp"), None),
            P(),
            P(None, "mp"),
            P(None, "mp"),
            P(("seq", "mp"), None),
            P(("seq", "mp")),
        ),
        out_specs=P(("seq", "mp"), None),
        check_vma=False,
    )
```

time: 88.2 us -> 63.6 us (0.72)
  the two profiles are of different devices: /device:TPU:16 before, /device:TPU:65 now
where the time goes in v2:
time: 63.6 us; the launch traced here: 63.5 us
  Pallas kernels  61.6 us (97%)
  local copies, waits for them, and re-layouts  1.87 us (3%)
    pallas_call x1, Pallas kernels, shards(): pl.pallas_call(kernel, out_shape=jax.ShapeDtypeStruct((TOKS, WIDTH), BF),...  61.6 us
    unnamed x1, local copies, waits for them, and re-layouts  1.87 us

profile of v2, /device:TPU:65, one launch (start us, length us, event | category | flops | bytes accessed | tf_op | source)
XLA Modules:
  0.0 63.5 jit_solution(7930868610651872794)
XLA Ops:
  0.0 61.6 %speech_window.1 = bf16[256,1024]{1,0:T(8,128)(2,1)} custom-call(bf16[1024,1024]{1,0:T(8,128)(2,1)} %frames_in.1, f32[31,1024]{1,0:T(8,128)} %taps_in.1, bf16[1024,128]{1,0:T(8,128)(2,1)} %key_panel.1, bf16[1024,128]{1,0:T(8,128)(2,1)} %value_panel.1, bf16[256,1024]{1,0:T(8,128)(2,1)} %queries_in.1, s32[1,256]{1,0:T(1,128)} %bitcast.1), custom_call_target="tpu_custom_call" | custom-call | flops 8999999488 | bytes 4500000 | tf_op jit(solution)/shard_map/speech_window/pallas_call | solution.py:505
  61.6 1.9 %copy.8 = bf16[256,1024]{1,0:T(8,128)(2,1)} copy(bf16[256,1024]{1,0:T(8,128)(2,1)} %speech_window.1) | data formatting | bytes 1048576

commit v3 on v2

--- a/solution.py
+++ b/solution.py
@@ -26,8 +26,8 @@
 CCOLS = WIDTH // CHUNKS
 NEG = -1e30
 SCALE2 = HEAD_DIM ** -0.5 * 1.4426950408889634
-FETCH_AT = 4
-OPEN_AT = 0
+FETCH_AT = 3
+EARLY_OWN = 0
 
 
 def kernel(
@@ -192,6 +192,8 @@
         off_p.start()
         off_o.start()
 
+    open_up()
+
     def band_bias(ref, first, row):
         count = ref.shape[0]
 
@@ -207,10 +209,6 @@
     band_bias(bias, me * ROWS, offown[0:1, :])
 
     def after_block(b):
-        @pl.when(b == OPEN_AT)
-        def _():
-            open_up()
-
         @pl.when(b == FETCH_AT)
         def _():
             fetched(1, True)
@@ -382,51 +380,6 @@
             o_copy(a).start()
             peaks = later
 
-    def chunk_step(g, _):
-        @pl.when(g == 0)
-        def _():
-            passed(2 + 2 * hi)
-            passed(3 + 2 * hi)
-
-        @pl.when(g == 1)
-        def _():
-            onward_queries(turn(-1))
-            passed(4 - 2 * hi)
-            passed(5 - 2 * hi)
-            fetched(6, False)
-            fetched(7, True)
-
-        @pl.when(g == 2)
-        def _():
-            passed(6)
-            passed(7)
-
-        @pl.when(g < CHUNKS - 1)
-        def _():
-            project_chunk(g + 1)
-
-        @pl.when(g == 0)
-        def _():
-            onward_queries(turn(2))
-
-        f_arrival(chunk_of(g)).wait_recv()
-        remote_chunk(chunk_of(g))
-
-        @pl.when(g == 1)
-        def _():
-            merge_chunk(turn(1))
-
-        @pl.when(g == 3)
-        def _():
-            merge_chunk(turn(0))
-            merge_chunk(turn(2))
-
-        return 0
-
-    project_chunk(0)
-    onward_queries(turn(1))
-    lax.fori_loop(0, CHUNKS, chunk_step, 0)
-
     def own_score(a, h):
         return score(kbuf[a], queries[:, panel_cols(a)], h, bias[...], score_refs[h])
 
@@ -435,21 +388,79 @@
         ctx[a, h * HEAD_DIM : (h + 1) * HEAD_DIM, :] = mixed
         near[a, 8 * h : 8 * h + 8, :] = jnp.concatenate([peak, total, jnp.zeros((6, TOKS), F32)], axis=0)
 
-    def own_step(a, peak0):
-        peak1 = own_score(a, 1)
-        weigh(score0, peak0, prob0)
-        own_mix(a, 0, peak0)
-        peak_next = own_score(jnp.minimum(a + 1, BLOCKS - 1), 0)
-        weigh(score1, peak1, prob1)
-        own_mix(a, 1, peak1)
-
-        @pl.when(a == 1)
+    def own_chunk(c):
+        peak = own_score(2 * c, 0)
+        for k in range(2):
+            a = 2 * c + k
+            peak1 = own_score(a, 1)
+            weigh(score0, peak, prob0)
+            own_mix(a, 0, peak)
+            if k == 0:
+                later = own_score(a + 1, 0)
+            weigh(score1, peak1, prob1)
+            own_mix(a, 1, peak1)
+            peak = later
+
+    def chunk_step(g, _):
+        @pl.when(g == 0)
+        def _():
+            passed(2 + 2 * hi)
+            passed(3 + 2 * hi)
+
+        @pl.when(g == 1)
+        def _():
+            onward_queries(turn(-1))
+            passed(6)
+            passed(7)
+
+        @pl.when(g < CHUNKS - 1)
+        def _():
+            project_chunk(g + 1)
+
+        @pl.when(g == 0)
+        def _():
+            fetched(6, False)
+            onward_queries(turn(2))
+            passed(4 - 2 * hi)
+            passed(5 - 2 * hi)
+            fetched(7, True)
+
+        @pl.when(g < EARLY_OWN)
+        def _():
+            own_chunk(chunk_of(g))
+
+        @pl.when(g == 3)
+        def _():
+            merge_chunk(turn(0))
+
+        f_arrival(chunk_of(g)).wait_recv()
+        remote_chunk(chunk_of(g))
+
+        @pl.when(g == 1)
+        def _():
+            merge_chunk(turn(1))
+
+        @pl.when(g == 3)
+        def _():
+            merge_chunk(turn(2))
+
+        return 0
+
+    project_chunk(0)
+    onward_queries(turn(1))
+    lax.fori_loop(0, CHUNKS, chunk_step, 0)
+
+    def late_own(g, _):
+        own_chunk(chunk_of(g))
+
+        @pl.when(g == EARLY_OWN)
         def _():
             merge_chunk(turn(-1))
 
-        return peak_next
-
-    lax.fori_loop(0, BLOCKS, own_step, own_score(0, 0))
+        return 0
+
+    lax.fori_loop(EARLY_OWN, CHUNKS, late_own, 0)
+
 
     def final_step(a, _):
         cols = pl.ds(pl.multiple_of(a * LANES, LANES), LANES)

time: 63.6 us -> 62.8 us (0.987)
  the two profiles are of different devices: /device:TPU:65 before, /device:TPU:1 now
where the time goes in v3:
time: 62.8 us; the launch traced here: 62.7 us
  Pallas kernels  60.8 us (97%)
  local copies, waits for them, and re-layouts  1.87 us (3%)
    pallas_call x1, Pallas kernels, shards(): pl.pallas_call(kernel, out_shape=jax.ShapeDtypeStruct((TOKS, WIDTH), BF),...  60.8 us
    unnamed x1, local copies, waits for them, and re-layouts  1.87 us

profile of v3, /device:TPU:1, one launch (start us, length us, event | category | flops | bytes accessed | tf_op | source)
XLA Modules:
  0.0 62.7 jit_solution(9068861988554208876)
XLA Ops:
  0.0 60.8 %speech_window.1 = bf16[256,1024]{1,0:T(8,128)(2,1)} custom-call(bf16[1024,1024]{1,0:T(8,128)(2,1)} %frames_in.1, f32[31,1024]{1,0:T(8,128)} %taps_in.1, bf16[1024,128]{1,0:T(8,128)(2,1)} %key_panel.1, bf16[1024,128]{1,0:T(8,128)(2,1)} %value_panel.1, bf16[256,1024]{1,0:T(8,128)(2,1)} %queries_in.1, s32[1,256]{1,0:T(1,128)} %bitcast.1), custom_call_target="tpu_custom_call" | custom-call | flops 8999999488 | bytes 4500000 | tf_op jit(solution)/shard_map/speech_window/pallas_call | solution.py:516
  60.8 1.9 %copy.8 = bf16[256,1024]{1,0:T(8,128)(2,1)} copy(bf16[256,1024]{1,0:T(8,128)(2,1)} %speech_window.1) | data formatting | bytes 1048576
